TPU v7x, 32 devices: a whole 2x2x4 slice. The times are simulated.
32 devices in a mesh: groups: 2 (over x), loop: 8 (over z, y), hid: 2 (over core).
Axes of the slice: x: 2, y: 2, z: 4, core: 2. Of those that a mesh axis runs over, the one named last changes fastest.
Arguments:
- tokens: bfloat16 [2048, 3072], P(('groups', 'loop')), parts along dimension 0, may hold values from -6 to 6
- cotangent: bfloat16 [2048, 3072], P(('groups', 'loop')), parts along dimension 0, may hold values from -6 to 6
- route_ids: int32 [16, 2], P('groups'), parts along dimension 0, may hold values from 0 to 7, as said below
- combine: float32 [2048], P(('groups', 'loop')), parts along dimension 0, may hold values from 0.1 to 1
- w_gate: bfloat16 [3072, 2048], P(None, ('loop', 'hid')), may hold values from -0.109375 to 0.109375
- w_up: bfloat16 [3072, 2048], P(None, ('loop', 'hid')), may hold values from -0.109375 to 0.109375
- w_down_t: bfloat16 [3072, 2048], P(None, ('loop', 'hid')), may hold values from -0.125 to 0.125
Outputs:
- mixed: bfloat16 [2048, 3072], P(('groups', 'loop'), 'hid'), parts along dimension 0
- tokens_grad: bfloat16 [2048, 3072], P(('groups', 'loop'), 'hid'), parts along dimension 0
There are 2 independent parts, one for each index of `groups`. A program takes and returns all parts, laid end to end along the dimension named above; an argument that names none is the same for every part. Nothing has to cross between parts.
Inputs may be any that keep to these rules, and one draw needn't show every extreme that they name: `route_ids`: each row names two different experts.
All inputs are finite; a program needn't handle non-finite values.
Results may differ from a plain program's by a relative error of at most 0.012.
Values may be sent and summed in bfloat16 or wider, within the bound.
A program may use at most 128 MiB of HBM per device.

v0:
```python
import jax
import jax.numpy as jnp
from jax import lax
from jax.sharding import PartitionSpec as P

BLOCK = 128


def from_partner(block, axis, distance):
    count = lax.axis_size(axis)
    route = []
    for low in range(count):
        high = low | 1 << distance
        if high != low and high < count:
            route += [(low, high), (high, low)]
    return lax.ppermute(block, axis, route)


def from_behind(block, axis, distance):
    devices = range(lax.axis_size(axis))
    route = [((i - distance) % len(devices), i) for i in devices]
    return lax.ppermute(block, axis, route)


def block_terms(stacked_weights, group_rows, routed_group, totals):
    weight_gate = stacked_weights[0]
    weight_up = stacked_weights[1]
    weight_down = stacked_weights[2]
    contract = (((1,), (1,)), ((), ()))

    def one_block(position, state):

        def compute(current):
            start = position * BLOCK
            inputs = lax.dynamic_slice_in_dim(group_rows[0], start, BLOCK, 0)
            scaled = lax.dynamic_slice_in_dim(group_rows[1], start, BLOCK, 0)
            gate = jnp.dot(inputs, weight_gate, preferred_element_type=jnp.float32)
            upward = jnp.dot(inputs, weight_up, preferred_element_type=jnp.float32)
            sigma = jax.nn.sigmoid(gate)
            active = gate * sigma
            hidden = (active * upward).astype(jnp.bfloat16)
            output_part = lax.dot_general(
                hidden, weight_down, contract, preferred_element_type=jnp.float32
            )
            grad_hidden = jnp.dot(scaled, weight_down, preferred_element_type=jnp.float32)
            grad_gate = (grad_hidden * upward * sigma * (1.0 + gate * (1.0 - sigma))).astype(
                jnp.bfloat16
            )
            grad_up = (grad_hidden * active).astype(jnp.bfloat16)
            input_part = lax.dot_general(
                grad_gate, weight_gate, contract, preferred_element_type=jnp.float32
            )
            input_part = input_part + lax.dot_general(
                grad_up, weight_up, contract, preferred_element_type=jnp.float32
            )
            previous = lax.dynamic_slice_in_dim(current, start, BLOCK, 1)
            return lax.dynamic_update_slice_in_dim(
                current, previous + jnp.stack([output_part, input_part]), start, 1
            )

        def keep_state(current):
            return current

        return lax.cond(routed_group[position] > 0, compute, keep_state, state)

    return lax.fori_loop(0, routed_group.shape[0], one_block, totals)


def split_halves(values, loop_index, bit):
    half_rows = values.shape[1] // 2
    upper_bit = loop_index >> bit & 1
    lower_part = values[:, :half_rows]
    upper_part = values[:, half_rows:]
    kept = jnp.where(upper_bit == 0, lower_part, upper_part)
    outgoing = jnp.where(upper_bit == 0, upper_part, lower_part)
    return (kept, outgoing)


def on_device(tokens, cotangent, route_ids, combine, w_gate, w_up, w_down_t):
    row_count = tokens.shape[0]
    blocks_here = row_count // BLOCK
    loop_index = lax.axis_index("loop")
    cycle_size = lax.axis_size("loop")
    routed = jnp.any(route_ids == 0, axis=1).astype(jnp.int32)
    local_routed = lax.dynamic_slice_in_dim(routed, loop_index * blocks_here, blocks_here)
    row_weight = combine * jnp.repeat(local_routed.astype(jnp.float32), BLOCK)
    scaled = (row_weight[:, None] * cotangent.astype(jnp.float32)).astype(jnp.bfloat16)
    group_rows = jnp.stack([tokens, scaled])
    for bit in range(2):
        partner = from_partner(group_rows, "loop", bit)
        upper_bit = loop_index >> bit & 1
        group_rows = jnp.where(
            upper_bit == 0,
            jnp.concatenate([group_rows, partner], 1),
            jnp.concatenate([partner, group_rows], 1),
        )
    group_start = loop_index // 4 * 4 * blocks_here
    routed_group = lax.dynamic_slice_in_dim(routed, group_start, 4 * blocks_here)
    totals = jnp.zeros((2, 4 * row_count, tokens.shape[1]), jnp.float32)
    weights = jnp.stack([w_gate, w_up, w_down_t])
    turns = cycle_size // 4

    def turn_once(step, carry):
        current, sums = carry
        sums = block_terms(current, group_rows, routed_group, sums)
        current = from_behind(current, "loop", 4)
        return (current, sums)

    weights, totals = lax.fori_loop(0, turns - 1, turn_once, (weights, totals))
    totals = block_terms(weights, group_rows, routed_group, totals)
    rounded = totals.astype(jnp.bfloat16)
    kept, outgoing = split_halves(rounded, loop_index, 1)
    received = from_partner(outgoing, "loop", 1)
    sums = kept.astype(jnp.float32) + received.astype(jnp.float32)
    kept, outgoing = split_halves(sums, loop_index, 0)
    sums = kept + from_partner(outgoing.astype(jnp.bfloat16), "loop", 0).astype(outgoing.dtype)
    sums = lax.psum_scatter(
        sums.astype(jnp.bfloat16), "hid", scatter_dimension=2, tiled=True
    ).astype(jnp.float32)
    mixed = (row_weight[:, None] * sums[0]).astype(jnp.bfloat16)
    tokens_grad = sums[1].astype(jnp.bfloat16)
    return (mixed, tokens_grad)


def solution(mesh):
    in_specs = (
        P(("groups", "loop"), None),
        P(("groups", "loop"), None),
        P("groups", None),
        P(("groups", "loop")),
        P(None, ("loop", "hid")),
        P(None, ("loop", "hid")),
        P(None, ("loop", "hid")),
    )
    out_specs = (P(("groups", "loop"), "hid"), P(("groups", "loop"), "hid"))
    return jax.shard_map(
        on_device, mesh=mesh, in_specs=in_specs, out_specs=out_specs, check_vma=False
    )
```

profile of v0, /device:TPU:0, one launch (start us, length us, event | category | flops | bytes accessed | tf_op | source)
XLA Modules:
  0.0 397.6 jit_solution(953838567700930105)
XLA Ops:
  7.2 0.7 compare_reduce_fusion
  7.9 0.6 dynamic_slice.46
  9.2 0.7 broadcast_multiply_fusion
  9.8 1.3 fusion.44
  11.2 2.5 pad_maximum_fusion.1
  13.6 3.0 collective-permute-start
  16.6 34.7 %collective-permute-done = bf16[2,128,3072]{2,1,0:T(8,128)(2,1)} collective-permute-done((bf16[2,128,3072]{2,1,0:T(8,128)(2,1)}, bf16[2,128,3072]{2,1,0:T(8,128)(2,1)}, u32[]{:S(2)}, u32[]{:S(2)}) %collective-permute-start) | collective-permute-done | bytes 1572896 | tf_op jit(solution)/shard_map/ppermute | solution.py:16
  51.3 4.0 %maximum_select_fusion.1 = bf16[2,256,3072]{2,1,0:T(8,128)(2,1)} fusion(bf16[2,128,3072]{2,1,0:T(8,128)(2,1)} %collective-permute-done, bf16[1,128,3072]{2,1,0:T(8,128)(2,1)S(1)} %fusion.44, bf16[1,128,3072]{2,1,0:T(8,128)(2,1)} %bitcast.66, pred[]{:T(512)S(6)} %eq.14), kind=kLoop, calls=%fused_computation.56 | loop fusion | flops 20447232 | bytes 6291457 | tf_op jit(solution)/shard_map/jit(_where)/select_n | solution.py:92
  55.3 1.8 collective-permute-start.1
  57.1 1.7 pad_maximum_fusion
  58.8 2.6 collective-permute-start.2
  61.5 113.0 %collective-permute-done.2 = bf16[3,3072,128]{2,1,0:T(8,128)(2,1)} collective-permute-done((bf16[3,3072,128]{2,1,0:T(8,128)(2,1)}, bf16[3,3072,128]{2,1,0:T(8,128)(2,1)}, u32[]{:S(2)}, u32[]{:S(2)}) %collective-permute-start.2) | collective-permute-done | bytes 2359328 | tf_op jit(solution)/shard_map/while/body/eval_jaxpr/ppermute | solution.py:22
  174.5 2.6 slice_bitcast_fusion
  177.1 9.7 %maximum_select_fusion = bf16[2,512,3072]{2,1,0:T(8,128)(2,1)} fusion(bf16[2,256,3072]{2,1,0:T(8,128)(2,1)} %collective-permute-done.1, bf16[2,256,3072]{2,1,0:T(8,128)(2,1)} %maximum_select_fusion.1, pred[]{:T(512)S(6)} %eq.15), kind=kLoop, calls=%fused_computation.54 | loop fusion | flops 28311552 | bytes 12582913 | tf_op jit(solution)/shard_map/jit(_where)/select_n | solution.py:92
  186.9 6.1 %broadcast_in_dim.2 = f32[2,512,3072]{2,1,0:T(8,128)} broadcast(f32[]{:T(128)} %constant.98.clone.1), dimensions={} | broadcast | bytes 12582916 | tf_op jit(solution)/shard_map/broadcast_in_dim | solution.py:99
  192.9 33.8 %while.40 = (s32[]{:T(128)}, f32[2,512,3072]{2,1,0:T(8,128)}, s32[4]{0:T(128)S(1)}, bf16[2,512,3072]{2,1,0:T(8,128)(2,1)}, bf16[3072,128]{1,0:T(8,128)(2,1)S(1)}...) while((s32[]{:T(128)}, f32[2,512,3072]{2,1,0:T(8,128)}, ...), condition=%wide.region_4.5_spmd, body=%wide.region_1.4_spmd.sunk | while | flops 606306304 | bytes 39190792 | solution.py:66
  194.1 0.6 dynamic_slice.76
  195.3 9.7 %conditional.4 = (f32[2,512,3072]{2,1,0:T(8,128)}) conditional(s32[]{:T(128)} %bitcast.60, f32[2,512,3072]{2,1,0:T(8,128)} %get-tuple-element.459, (s32[]{:T(128)}, f32[2,512,3072]{2,1,0:T(8,128)}, bf16[2,512,3072]{2,1,0:T(8,128)(2,1)}, bf16[3072,128]{1,0:T(8,128)(2,1)S(1)}, bf16[3072,128]{1,0:T(8,128)(2,1)}, ...), branch_computations={%region_2.2_spmd, %region_3.3_spmd} | conditional | flops 606306304 | bytes 39190624 | solution.py:64
  195.4 3.4 fusion.46
  200.9 4.1 %fusion.1 = f32[2,512,3072]{2,1,0:T(8,128)} fusion(f32[2,512,3072]{2,1,0:T(8,128)} %get-tuple-element.294, s32[]{:T(128)S(6)} %select_n.56, f32[1,128,3072]{2,1,0:T(8,128)S(1)} %fusion, f32[1,128,3072]{2,1,0:T(8,128)S(1)} %convolution_bitcast_fusion), kind=kLoop, calls=%fused_computation.4 | loop fusion | flops 1572864 | bytes 9437188 | tf_op jit(solution)/shard_map/while/body/eval_jaxpr/while/body/eval_jaxpr/cond/branch_1_fun/dynamic_update_slice | solution.py:57
  206.2 9.7 %conditional.4 = (f32[2,512,3072]{2,1,0:T(8,128)}) conditional(s32[]{:T(128)} %bitcast.60, f32[2,512,3072]{2,1,0:T(8,128)} %get-tuple-element.459, (s32[]{:T(128)}, f32[2,512,3072]{2,1,0:T(8,128)}, bf16[2,512,3072]{2,1,0:T(8,128)(2,1)}, bf16[3072,128]{1,0:T(8,128)(2,1)S(1)}, bf16[3072,128]{1,0:T(8,128)(2,1)}, ...), branch_computations={%region_2.2_spmd, %region_3.3_spmd} | conditional | flops 606306304 | bytes 39190624 | solution.py:64
  206.3 3.4 fusion.46
  211.8 4.1 %fusion.1 = f32[2,512,3072]{2,1,0:T(8,128)} fusion(f32[2,512,3072]{2,1,0:T(8,128)} %get-tuple-element.294, s32[]{:T(128)S(6)} %select_n.56, f32[1,128,3072]{2,1,0:T(8,128)S(1)} %fusion, f32[1,128,3072]{2,1,0:T(8,128)S(1)} %convolution_bitcast_fusion), kind=kLoop, calls=%fused_computation.4 | loop fusion | flops 1572864 | bytes 9437188 | tf_op jit(solution)/shard_map/while/body/eval_jaxpr/while/body/eval_jaxpr/cond/branch_1_fun/dynamic_update_slice | solution.py:57
  217.0 9.7 %conditional.4 = (f32[2,512,3072]{2,1,0:T(8,128)}) conditional(s32[]{:T(128)} %bitcast.60, f32[2,512,3072]{2,1,0:T(8,128)} %get-tuple-element.459, (s32[]{:T(128)}, f32[2,512,3072]{2,1,0:T(8,128)}, bf16[2,512,3072]{2,1,0:T(8,128)(2,1)}, bf16[3072,128]{1,0:T(8,128)(2,1)S(1)}, bf16[3072,128]{1,0:T(8,128)(2,1)}, ...), branch_computations={%region_2.2_spmd, %region_3.3_spmd} | conditional | flops 606306304 | bytes 39190624 | solution.py:64
  217.1 3.4 fusion.46
  222.7 4.1 %fusion.1 = f32[2,512,3072]{2,1,0:T(8,128)} fusion(f32[2,512,3072]{2,1,0:T(8,128)} %get-tuple-element.294, s32[]{:T(128)S(6)} %select_n.56, f32[1,128,3072]{2,1,0:T(8,128)S(1)} %fusion, f32[1,128,3072]{2,1,0:T(8,128)S(1)} %convolution_bitcast_fusion), kind=kLoop, calls=%fused_computation.4 | loop fusion | flops 1572864 | bytes 9437188 | tf_op jit(solution)/shard_map/while/body/eval_jaxpr/while/body/eval_jaxpr/cond/branch_1_fun/dynamic_update_slice | solution.py:57
  226.7 34.1 %while.41 = (s32[]{:T(128)}, f32[2,512,3072]{2,1,0:T(8,128)}, s32[4]{0:T(128)S(1)}, bf16[2,512,3072]{2,1,0:T(8,128)(2,1)}, bf16[3072,128]{1,0:T(8,128)(2,1)S(1)}...) while((s32[]{:T(128)}, f32[2,512,3072]{2,1,0:T(8,128)}, ...), condition=%wide.region_8.9_spmd, body=%wide.region_5.8_spmd.sunk | while | flops 606306304 | bytes 39190792 | solution.py:66
  228.0 0.6 dynamic_slice.77
  229.2 9.7 %conditional.5 = (f32[2,512,3072]{2,1,0:T(8,128)}) conditional(s32[]{:T(128)} %bitcast.61, f32[2,512,3072]{2,1,0:T(8,128)} %get-tuple-element.486, (s32[]{:T(128)}, f32[2,512,3072]{2,1,0:T(8,128)}, bf16[2,512,3072]{2,1,0:T(8,128)(2,1)}, bf16[3072,128]{1,0:T(8,128)(2,1)S(1)}, bf16[3072,128]{1,0:T(8,128)(2,1)}, ...), branch_computations={%region_6.6_spmd, %region_7.7_spmd} | conditional | flops 606306304 | bytes 39190624 | solution.py:64
  229.3 3.4 fusion.47
  234.8 4.1 %fusion.23 = f32[2,512,3072]{2,1,0:T(8,128)} fusion(f32[2,512,3072]{2,1,0:T(8,128)} %get-tuple-element.308, s32[]{:T(128)S(6)} %select_n.57, f32[1,128,3072]{2,1,0:T(8,128)S(1)} %fusion.22, f32[1,128,3072]{2,1,0:T(8,128)S(1)} %convolution_bitcast_fusion.1), kind=kLoop, calls=%fused_computation.31 | loop fusion | flops 1572864 | bytes 9437188 | tf_op jit(solution)/shard_map/while/body/eval_jaxpr/cond/branch_1_fun/dynamic_update_slice | solution.py:57
  240.2 9.7 %conditional.5 = (f32[2,512,3072]{2,1,0:T(8,128)}) conditional(s32[]{:T(128)} %bitcast.61, f32[2,512,3072]{2,1,0:T(8,128)} %get-tuple-element.486, (s32[]{:T(128)}, f32[2,512,3072]{2,1,0:T(8,128)}, bf16[2,512,3072]{2,1,0:T(8,128)(2,1)}, bf16[3072,128]{1,0:T(8,128)(2,1)S(1)}, bf16[3072,128]{1,0:T(8,128)(2,1)}, ...), branch_computations={%region_6.6_spmd, %region_7.7_spmd} | conditional | flops 606306304 | bytes 39190624 | solution.py:64
  240.2 3.4 fusion.47
  245.8 4.1 %fusion.23 = f32[2,512,3072]{2,1,0:T(8,128)} fusion(f32[2,512,3072]{2,1,0:T(8,128)} %get-tuple-element.308, s32[]{:T(128)S(6)} %select_n.57, f32[1,128,3072]{2,1,0:T(8,128)S(1)} %fusion.22, f32[1,128,3072]{2,1,0:T(8,128)S(1)} %convolution_bitcast_fusion.1), kind=kLoop, calls=%fused_computation.31 | loop fusion | flops 1572864 | bytes 9437188 | tf_op jit(solution)/shard_map/while/body/eval_jaxpr/cond/branch_1_fun/dynamic_update_slice | solution.py:57
  251.1 9.7 %conditional.5 = (f32[2,512,3072]{2,1,0:T(8,128)}) conditional(s32[]{:T(128)} %bitcast.61, f32[2,512,3072]{2,1,0:T(8,128)} %get-tuple-element.486, (s32[]{:T(128)}, f32[2,512,3072]{2,1,0:T(8,128)}, bf16[2,512,3072]{2,1,0:T(8,128)(2,1)}, bf16[3072,128]{1,0:T(8,128)(2,1)S(1)}, bf16[3072,128]{1,0:T(8,128)(2,1)}, ...), branch_computations={%region_6.6_spmd, %region_7.7_spmd} | conditional | flops 606306304 | bytes 39190624 | solution.py:64
  251.1 3.4 fusion.47
  256.7 4.1 %fusion.23 = f32[2,512,3072]{2,1,0:T(8,128)} fusion(f32[2,512,3072]{2,1,0:T(8,128)} %get-tuple-element.308, s32[]{:T(128)S(6)} %select_n.57, f32[1,128,3072]{2,1,0:T(8,128)S(1)} %fusion.22, f32[1,128,3072]{2,1,0:T(8,128)S(1)} %convolution_bitcast_fusion.1), kind=kLoop, calls=%fused_computation.31 | loop fusion | flops 1572864 | bytes 9437188 | tf_op jit(solution)/shard_map/while/body/eval_jaxpr/cond/branch_1_fun/dynamic_update_slice | solution.py:57
  260.8 8.1 %convert_element_type.83 = bf16[2,512,3072]{2,1,0:T(8,128)(2,1)} convert(f32[2,512,3072]{2,1,0:T(8,128)} %get-tuple-element.327) | non-fusion elementwise | flops 3145728 | bytes 18874368 | tf_op jit(solution)/shard_map/convert_element_type | solution.py:111
  268.9 3.3 broadcast_select_fusion
  272.2 3.6 collective-permute-start.3
  275.8 66.3 %collective-permute-done.3 = bf16[2,256,3072]{2,1,0:T(8,128)(2,1)S(1)} collective-permute-done((bf16[2,256,3072]{2,1,0:T(8,128)(2,1)S(1)}, bf16[2,256,3072]{2,1,0:T(8,128)(2,1)S(1)}, u32[]{:S(2)}, u32[]{:S(2)}) %collective-permute-start.3) | collective-permute-done | bytes 3145760 | tf_op jit(solution)/shard_map/ppermute | solution.py:16
  342.1 1.7 convert_add_fusion
  344.1 1.6 collective-permute-start.4
  345.7 32.2 %collective-permute-done.4 = bf16[2,128,3072]{2,1,0:T(8,128)(2,1)S(1)} collective-permute-done((bf16[2,128,3072]{2,1,0:T(8,128)(2,1)S(1)}, bf16[2,128,3072]{2,1,0:T(8,128)(2,1)S(1)}, u32[]{:S(2)}, u32[]{:S(2)}) %collective-permute-start.4) | collective-permute-done | bytes 1572896 | tf_op jit(solution)/shard_map/ppermute | solution.py:16
  377.8 1.9 add_convert_fusion
  379.8 7.4 %reduce-scatter.2.cloned.1.call-done = bf16[2,128,1536]{2,1,0:T(8,128)(2,1)} async-done(((bf16[2,128,3072]{2,1,0:T(8,128)(2,1)}), bf16[2,128,1536]{2,1,0:T(8,128)(2,1)}) %reduce-scatter.2.cloned.1.call-update) | async-done | bytes 786448 | tf_op jit(solution)/shard_map/reduce_scatter | solution.py:117
  387.2 1.9 fusion.45
  389.0 1.8 slice_bitcast_fusion.3
  (70 shorter events, 17.0 us)
Async XLA Ops:
  7.2 380.0 %reduce-scatter.2.cloned.1.call-start = ((), (), s32[]{:S(2)}) async-start(), calls=%async_computation.1 | async-start | bytes 2359296 | tf_op jit(solution)/shard_map/reduce_scatter | solution.py:117
  13.6 37.7 %collective-permute-start = (bf16[2,128,3072]{2,1,0:T(8,128)(2,1)}, bf16[2,128,3072]{2,1,0:T(8,128)(2,1)}, u32[]{:S(2)}, u32[]{:S(2)}) collective-permute-start(bf16[2,128,3072]{2,1,0:T(8,128)(2,1)} %pad_maximum_fusion.1), channel_id=1, source_target_pairs={{0,2},{2,0},{4,6},{6,4},{8,10},{10,8},{12,14},{14,12},{1,3},{3,1},... | collective-permute-start | bytes 4718600 | tf_op jit(solution)/shard_map/ppermute | solution.py:16
  16.6 40.5 %copy-start = (bf16[3072,128]{1,0:T(8,128)(2,1)S(1)}, bf16[3072,128]{1,0:T(8,128)(2,1)}, u32[]{:S(2)}) copy-start(bf16[3072,128]{1,0:T(8,128)(2,1)} %param.21) | copy-start | bytes 2359300
  16.6 40.5 %copy-start.1 = (bf16[3072,128]{1,0:T(8,128)(2,1)S(1)}, bf16[3072,128]{1,0:T(8,128)(2,1)}, u32[]{:S(2)}) copy-start(bf16[3072,128]{1,0:T(8,128)(2,1)} %param.19) | copy-start | bytes 2359300
  16.6 40.5 %copy-start.2 = (bf16[3072,128]{1,0:T(8,128)(2,1)S(1)}, bf16[3072,128]{1,0:T(8,128)(2,1)}, u32[]{:S(2)}) copy-start(bf16[3072,128]{1,0:T(8,128)(2,1)} %param.20) | copy-start | bytes 2359300
  55.3 121.8 %collective-permute-start.1 = (bf16[2,256,3072]{2,1,0:T(8,128)(2,1)}, bf16[2,256,3072]{2,1,0:T(8,128)(2,1)}, u32[]{:S(2)}, u32[]{:S(2)}) collective-permute-start(bf16[2,256,3072]{2,1,0:T(8,128)(2,1)} %maximum_select_fusion.1), channel_id=1, source_target_pairs={{0,4},{4,0},{2,6},{6,2},{8,12},{12,8},{10,14},{14,10},{1,5},{5,1},... | collective-permute-start | bytes 9437192 | tf_op jit(solution)/shard_map/ppermute | solution.py:16
  58.8 115.6 %collective-permute-start.2 = (bf16[3,3072,128]{2,1,0:T(8,128)(2,1)}, bf16[3,3072,128]{2,1,0:T(8,128)(2,1)}, u32[]{:S(2)}, u32[]{:S(2)}) collective-permute-start(bf16[3,3072,128]{2,1,0:T(8,128)(2,1)} %pad_maximum_fusion), channel_id=1, source_target_pairs={{8,0},{10,2},{12,4},{14,6},{0,8},{2,10},{4,12},{6,14},{9,1},{11,3}... | collective-permute-start | bytes 7077896 | tf_op jit(solution)/shard_map/while/body/eval_jaxpr/ppermute | solution.py:22
  195.3 3.7 copy-start.3
  206.2 3.7 copy-start.3
  217.1 3.7 copy-start.3
  229.3 3.7 copy-start.4
  240.2 3.7 copy-start.4
  251.1 3.7 copy-start.4
  268.9 73.2 %copy-start.5 = (bf16[2,512,3072]{2,1,0:T(8,128)(2,1)S(1)}, bf16[2,512,3072]{2,1,0:T(8,128)(2,1)}, u32[]{:S(2)}) copy-start(bf16[2,512,3072]{2,1,0:T(8,128)(2,1)} %convert_element_type.83) | copy-start | bytes 18874372
  272.2 69.9 %collective-permute-start.3 = (bf16[2,256,3072]{2,1,0:T(8,128)(2,1)S(1)}, bf16[2,256,3072]{2,1,0:T(8,128)(2,1)S(1)}, u32[]{:S(2)}, u32[]{:S(2)}) collective-permute-start(bf16[2,256,3072]{2,1,0:T(8,128)(2,1)S(1)} %broadcast_select_fusion), channel_id=1, source_target_pairs={{0,4},{4,0},{2,6},{6,2},{8,12},{12,8},{10,14},{14,10},{1,5},{5,1},... | collective-permute-start | bytes 9437192 | tf_op jit(solution)/shard_map/ppermute | solution.py:16
  344.1 33.8 %collective-permute-start.4 = (bf16[2,128,3072]{2,1,0:T(8,128)(2,1)S(1)}, bf16[2,128,3072]{2,1,0:T(8,128)(2,1)S(1)}, u32[]{:S(2)}, u32[]{:S(2)}) collective-permute-start(bf16[2,128,3072]{2,1,0:T(8,128)(2,1)S(1)} %select_convert_fusion), channel_id=1, source_target_pairs={{0,2},{2,0},{4,6},{6,4},{8,10},{10,8},{12,14},{14,12},{1,3},{3,1},... | collective-permute-start | bytes 4718600 | tf_op jit(solution)/shard_map/ppermute | solution.py:16
Sparse Core Ops, SparseCore 0:
  379.9 7.2 reduce-scatter.1
where the time goes:
time: 398 us
  waiting for transfers between devices  254 us (64%)
  other arithmetic  62.3 us (16%)
  local copies, waits for them, and re-layouts  36 us (9%)
  between operations  14.7 us (4%)
  matrix products  13 us (3%)
  starting transfers between devices  12.5 us (3%)
  loops' own time  5.47 us (1%)
    ppermute x4, waiting for transfers between devices, from_partner(): return lax.ppermute(block, axis, route)  133 us
    ppermute x1, waiting for transfers between devices, from_behind(): return lax.ppermute(block, axis, route)  113 us
    dynamic_update_slice x6, other arithmetic, compute(): lax.dynamic_update_slice_in_dim(current, previous + jnp.stack([output_par...  24.5 us
    slice x6, local copies, waits for them, and re-layouts, compute(): scaled = lax.dynamic_slice_in_dim(group_rows[1], start, BLOCK, 0)  20.1 us
    select_n x2, other arithmetic, on_device(): jnp.where(upper_bit == 0, jnp.concatenate([group_rows, partner], 1), jnp....  13.7 us
    ppermute x4, starting transfers between devices, from_partner(): return lax.ppermute(block, axis, route)  9.91 us
    convert_element_type x1, other arithmetic, on_device(): rounded = totals.astype(jnp.bfloat16)  8.14 us
  transfers between devices with their start and end apart: 6, of which 5 were waited for; matrix products, arithmetic and copies ran while one was open for 1% of the time, Pallas kernels for 0%

commit v1 on v0

--- a/solution.py
+++ b/solution.py
@@ -1,9 +1,418 @@
+import functools
+
 import jax
 import jax.numpy as jnp
 from jax import lax
+from jax.experimental import pallas as pl
+from jax.experimental.pallas import tpu as pltpu
 from jax.sharding import PartitionSpec as P
 
 BLOCK = 128
+PARTS_OF_WEIGHT = 2
+MESH = pl.DeviceIdType.MESH
+
+
+def line_kernel(
+    line, route_ref, combine_ref, tokens_ref, cotangent_ref, gate_ref, up_ref, down_ref,
+    mixed_ref, grad_ref,
+    weights, rows_in, cotan, hidden, sums, from_left, from_right, total, swap_out, swap_in,
+    own_sem, gather_send, gather_recv,
+    sibling_send, sibling_recv, side_send, side_recv, cross_send, cross_recv,
+    relay_send, relay_recv, left_send, left_recv, right_recv, swap_send, swap_recv,
+):
+    group = lax.axis_index("groups")
+    loop = lax.axis_index("loop")
+    core = lax.axis_index("hid")
+    place = loop // 2
+    half = rows_in.shape[2]
+    width = rows_in.shape[3]
+    units = gate_ref.shape[1]
+    chunk = width // 2
+    sibling = {"hid": 1 - core}
+    side = {"loop": loop + 1 - 2 * lax.rem(loop, 2)}
+    cross = {"groups": 1 - group}
+    left = {"loop": loop - 2}
+    right = {"loop": loop + 2}
+    has_left = place > 0
+    has_right = place < line - 1
+    sources = (gate_ref, up_ref, down_ref)
+    my_rows = pl.ds(pl.multiple_of(core * half, half), half)
+
+    barrier = pltpu.get_barrier_semaphore()
+    for other in (sibling, side, cross):
+        pl.semaphore_signal(barrier, inc=1, device_id=other, device_id_type=MESH)
+
+    @pl.when(has_left)
+    def _():
+        pl.semaphore_signal(barrier, inc=1, device_id=left, device_id_type=MESH)
+
+    @pl.when(has_right)
+    def _():
+        pl.semaphore_signal(barrier, inc=1, device_id=right, device_id_type=MESH)
+
+    own = [
+        pltpu.make_async_copy(cotangent_ref.at[my_rows, :], cotan, own_sem.at[0]),
+        pltpu.make_async_copy(tokens_ref.at[my_rows, :], rows_in.at[place, 0], own_sem.at[1]),
+    ]
+    for m in range(3):
+        own.append(
+            pltpu.make_async_copy(sources[m], weights.at[m, :, pl.ds(0, units)], own_sem.at[2 + m])
+        )
+    for copy in own:
+        copy.start()
+
+    @pl.when(has_left & has_right)
+    def _():
+        pl.semaphore_wait(barrier, 5)
+
+    @pl.when(jnp.logical_not(has_left & has_right))
+    def _():
+        pl.semaphore_wait(barrier, 4)
+
+    def remote(src, dst, send, recv, other):
+        return pltpu.make_async_remote_copy(
+            src_ref=src, dst_ref=dst, send_sem=send, recv_sem=recv,
+            device_id=other, device_id_type=MESH,
+        )
+
+    def gather_copy(block, kind, way):
+        other = left if way == 0 else right
+        ref = rows_in.at[block, kind]
+        return remote(
+            ref, ref, gather_send.at[way, block, kind], gather_recv.at[block, kind], other
+        )
+
+    def send_both(kind):
+        @pl.when(has_left)
+        def _():
+            gather_copy(place, kind, 0).start()
+
+        @pl.when(has_right)
+        def _():
+            gather_copy(place, kind, 1).start()
+
+    piece = width // 2 // PARTS_OF_WEIGHT
+
+    def piece_rows(part_half, i):
+        return pl.ds(pl.multiple_of(part_half * (width // 2) + i * piece, piece), piece)
+
+    def side_copy(m, i):
+        rows = piece_rows(group, i)
+        return remote(
+            sources[m].at[rows, :], weights.at[m, rows, pl.ds(2 * units, units)],
+            side_send.at[m, i], side_recv.at[m, i], side,
+        )
+
+    def cross_copy(m, i, part_half):
+        ref = weights.at[m, piece_rows(part_half, i), pl.ds(2 * units, units)]
+        return remote(ref, ref, cross_send.at[m, i], cross_recv.at[m, i], cross)
+
+    def relay_copy(m, i, late):
+        rows = piece_rows(group if late == 0 else 1 - group, i)
+        return remote(
+            weights.at[m, rows, pl.ds(2 * units, units)],
+            weights.at[m, rows, pl.ds(3 * units, units)],
+            relay_send.at[late, m, i], relay_recv.at[late, m, i], sibling,
+        )
+
+    def sibling_copy(m):
+        return remote(
+            sources[m], weights.at[m, :, pl.ds(units, units)],
+            sibling_send.at[m], sibling_recv.at[m], sibling,
+        )
+
+    for m in range(3):
+        for i in range(PARTS_OF_WEIGHT):
+            side_copy(m, i).start()
+    own[1].wait()
+    send_both(0)
+
+    chosen = (route_ref[loop, 0] == 0) | (route_ref[loop, 1] == 0)
+    flag = jnp.where(chosen, 1.0, 0.0)
+    lanes = lax.broadcasted_iota(jnp.int32, (half, 2 * half), 1)
+    heights = lax.broadcasted_iota(jnp.int32, (half, 2 * half), 0) + core * half
+    picked = jnp.where(lanes == heights, combine_ref[...], 0.0)
+    row_weight = jnp.sum(picked, axis=1, keepdims=True) * flag
+    own[0].wait()
+    rows_in[place, 1] = (row_weight * cotan[...].astype(jnp.float32)).astype(jnp.bfloat16)
+    send_both(1)
+    for m in range(3):
+        sibling_copy(m).start()
+
+    def pass_on(distance, kind):
+        @pl.when((place - distance >= 0) & has_right)
+        def _():
+            gather_copy(place - distance, kind, 1).wait_recv()
+            gather_copy(place - distance, kind, 1).start()
+
+        @pl.when((place + distance < line) & has_left)
+        def _():
+            gather_copy(place + distance, kind, 0).wait_recv()
+            gather_copy(place + distance, kind, 0).start()
+
+    relays = [(d, kind) for d in range(1, line - 1) for kind in range(2)]
+    pieces = [(m, i) for m in range(3) for i in range(PARTS_OF_WEIGHT)]
+    for step, (m, i) in enumerate(pieces):
+        side_copy(m, i).wait_recv()
+        cross_copy(m, i, group).start()
+        relay_copy(m, i, 0).start()
+        if step % 2 == 1 and relays:
+            pass_on(*relays.pop(0))
+        if step >= 1:
+            mm, ii = pieces[step - 1]
+            cross_copy(mm, ii, 1 - group).wait_recv()
+            relay_copy(mm, ii, 1).start()
+    mm, ii = pieces[-1]
+    cross_copy(mm, ii, 1 - group).wait_recv()
+    relay_copy(mm, ii, 1).start()
+    while relays:
+        pass_on(*relays.pop(0))
+    for m in range(3):
+        own[2 + m].wait()
+        sibling_copy(m).wait_recv()
+        for i in range(PARTS_OF_WEIGHT):
+            relay_copy(m, i, 0).wait_recv()
+            relay_copy(m, i, 1).wait_recv()
+
+    contract = (((1,), (1,)), ((), ()))
+
+    def terms(block):
+        def first(t, _):
+            cols = pl.ds(pl.multiple_of(t * 256, 256), 256)
+            gate = jnp.dot(rows_in[block, 0], weights[0, :, cols], preferred_element_type=jnp.float32)
+            upward = jnp.dot(rows_in[block, 0], weights[1, :, cols], preferred_element_type=jnp.float32)
+            grad_hidden = jnp.dot(
+                rows_in[block, 1], weights[2, :, cols], preferred_element_type=jnp.float32
+            )
+            sigma = jax.nn.sigmoid(gate)
+            active = gate * sigma
+            hidden[0, :, cols] = (active * upward).astype(jnp.bfloat16)
+            hidden[1, :, cols] = (
+                grad_hidden * upward * sigma * (1.0 + gate * (1.0 - sigma))
+            ).astype(jnp.bfloat16)
+            hidden[2, :, cols] = (grad_hidden * active).astype(jnp.bfloat16)
+            return 0
+
+        lax.fori_loop(0, weights.shape[2] // 256, first, 0)
+
+        def second(t, _):
+            cols = pl.ds(pl.multiple_of(t * 512, 512), 512)
+            output_part = lax.dot_general(
+                hidden[0], weights[2, cols, :], contract, preferred_element_type=jnp.float32
+            )
+            sums[block, 0, :, cols] = output_part.astype(jnp.bfloat16)
+            input_part = lax.dot_general(
+                hidden[1], weights[0, cols, :], contract, preferred_element_type=jnp.float32
+            ) + lax.dot_general(
+                hidden[2], weights[1, cols, :], contract, preferred_element_type=jnp.float32
+            )
+            sums[block, 1, :, cols] = input_part.astype(jnp.bfloat16)
+            return 0
+
+        lax.fori_loop(0, width // 512, second, 0)
+
+    def sum_copy(block, kind, part, way):
+        cols = pl.ds(part * chunk, chunk)
+        target = from_right if way == 0 else from_left
+        recv = right_recv if way == 0 else left_recv
+        return remote(
+            sums.at[block, kind, :, cols], target.at[block, kind, :, cols],
+            left_send.at[block, kind, part], recv.at[block, kind, part],
+            left if way == 0 else right,
+        )
+
+    quarters = [(kind, part) for kind in range(2) for part in range(2)]
+
+    def one_block(index, _):
+        distance = (index + 2) // 2
+        way = lax.rem(index, 2)
+        apart = jnp.where(index == 2 * (line - 1), 0, distance * (2 * way - 1))
+        block = place + apart
+
+        @pl.when((block >= 0) & (block < line))
+        def _():
+            @pl.when(jnp.logical_not(has_left) & (apart > 0))
+            def _():
+                for kind in range(2):
+                    gather_copy(block, kind, 0).wait_recv()
+
+            @pl.when(jnp.logical_not(has_right) & (apart < 0))
+            def _():
+                for kind in range(2):
+                    gather_copy(block, kind, 1).wait_recv()
+
+            terms(block)
+
+            @pl.when(jnp.logical_not(has_left) & (apart > 0))
+            def _():
+                for kind, part in quarters:
+                    sum_copy(block, kind, part, 1).start()
+
+            @pl.when(jnp.logical_not(has_right) & (apart < 0))
+            def _():
+                for kind, part in quarters:
+                    sum_copy(block, kind, part, 0).start()
+
+        return 0
+
+    lax.fori_loop(0, 2 * (line - 1) + 1, one_block, 0)
+
+    def merge(block, kind, part, arrived):
+        cols = pl.ds(part * chunk, chunk)
+        sums[block, kind, :, cols] = (
+            sums[block, kind, :, cols].astype(jnp.float32)
+            + arrived[block, kind, :, cols].astype(jnp.float32)
+        ).astype(jnp.bfloat16)
+
+    def forward(block, kind, part, way):
+        sum_copy(block, kind, part, way).wait_recv()
+        merge(block, kind, part, from_left if way == 1 else from_right)
+        sum_copy(block, kind, part, way).start()
+
+    low = place < line // 2
+
+    def onward(turn, _):
+        to_right = has_left & (turn > place)
+        to_left = has_right & (line - 1 - turn < place)
+        for kind, part in quarters:
+            @pl.when(to_right & low)
+            def _():
+                forward(turn, kind, part, 1)
+
+            @pl.when(to_left)
+            def _():
+                forward(line - 1 - turn, kind, part, 0)
+
+            @pl.when(to_right & jnp.logical_not(low))
+            def _():
+                forward(turn, kind, part, 1)
+        return 0
+
+    lax.fori_loop(1, line, onward, 0)
+
+    outputs = (mixed_ref, grad_ref)
+
+    def swap_copy(kind):
+        return remote(
+            swap_out.at[kind], swap_in.at[kind], swap_send.at[kind], swap_recv.at[kind], sibling
+        )
+
+    for kind in range(2):
+        for part in range(2):
+            cols = pl.ds(part * chunk, chunk)
+            total[...] = sums[place, kind, :, cols].astype(jnp.float32)
+
+            @pl.when(has_left)
+            def _():
+                sum_copy(place, kind, part, 1).wait_recv()
+                total[...] += from_left[place, kind, :, cols].astype(jnp.float32)
+
+            @pl.when(has_right)
+            def _():
+                sum_copy(place, kind, part, 0).wait_recv()
+                total[...] += from_right[place, kind, :, cols].astype(jnp.float32)
+
+            value = total[...]
+            if kind == 0:
+                value = row_weight * value
+            value = value.astype(jnp.bfloat16)
+
+            @pl.when(core == part)
+            def _():
+                outputs[kind][my_rows, :] = value
+
+            @pl.when(core != part)
+            def _():
+                swap_out[kind] = value
+        swap_copy(kind).start()
+    other_rows = pl.ds(pl.multiple_of((1 - core) * half, half), half)
+    for kind in range(2):
+        swap_copy(kind).wait_recv()
+        outputs[kind][other_rows, :] = swap_in[kind]
+
+    for kind in range(2):
+        swap_copy(kind).wait_send()
+    for m in range(3):
+        sibling_copy(m).wait_send()
+        for i in range(PARTS_OF_WEIGHT):
+            side_copy(m, i).wait_send()
+            cross_copy(m, i, group).wait_send()
+            relay_copy(m, i, 0).wait_send()
+            relay_copy(m, i, 1).wait_send()
+
+    def settle(block, _):
+        @pl.when(has_left & (block >= place))
+        def _():
+            for kind in range(2):
+                gather_copy(block, kind, 0).wait_send()
+
+        @pl.when(has_right & (block <= place))
+        def _():
+            for kind in range(2):
+                gather_copy(block, kind, 1).wait_send()
+
+        @pl.when(block != place)
+        def _():
+            for kind, part in quarters:
+                sum_copy(block, kind, part, 0).wait_send()
+        return 0
+
+    lax.fori_loop(0, line, settle, 0)
+
+
+def on_line(tokens, cotangent, route_ids, combine, w_gate, w_up, w_down_t):
+    rows, width = tokens.shape
+    units = w_gate.shape[1]
+    half = rows // 2
+    line = lax.axis_size("loop") // 2
+    any_space = pl.BlockSpec(memory_space=pl.ANY)
+    vmem = pl.BlockSpec(memory_space=pltpu.VMEM)
+    bf16 = jnp.bfloat16
+    dma = pltpu.SemaphoreType.DMA
+    pieces = PARTS_OF_WEIGHT
+    out = jax.ShapeDtypeStruct((rows, width // 2), bf16)
+    return pl.pallas_call(
+        functools.partial(line_kernel, line),
+        out_shape=(out, out),
+        in_specs=[pl.BlockSpec(memory_space=pltpu.SMEM), vmem] + [any_space] * 5,
+        out_specs=(vmem, vmem),
+        scratch_shapes=[
+            pltpu.VMEM((3, width, 4 * units), bf16),
+            pltpu.VMEM((line, 2, half, width), bf16),
+            pltpu.VMEM((half, width), bf16),
+            pltpu.VMEM((3, half, 4 * units), bf16),
+            pltpu.VMEM((line, 2, half, width), bf16),
+            pltpu.VMEM((line, 2, half, width), bf16),
+            pltpu.VMEM((line, 2, half, width), bf16),
+            pltpu.VMEM((half, width // 2), jnp.float32),
+            pltpu.VMEM((2, half, width // 2), bf16),
+            pltpu.VMEM((2, half, width // 2), bf16),
+            dma((5,)),
+            dma((2, line, 2)),
+            dma((line, 2)),
+            dma((3,)),
+            dma((3,)),
+            dma((3, pieces)),
+            dma((3, pieces)),
+            dma((3, pieces)),
+            dma((3, pieces)),
+            dma((2, 3, pieces)),
+            dma((2, 3, pieces)),
+            dma((line, 2, 2)),
+            dma((line, 2, 2)),
+            dma((line, 2, 2)),
+            dma((2,)),
+            dma((2,)),
+        ],
+        compiler_params=pltpu.CompilerParams(
+            collective_id=0, has_side_effects=True, vmem_limit_bytes=48 * 1024 * 1024
+        ),
+        cost_estimate=pl.CostEstimate(
+            flops=12 * line * half * width * 4 * units,
+            bytes_accessed=2 * (3 * width * units + 3 * rows * width),
+            transcendentals=line * half * 4 * units,
+        ),
+    )(route_ids, combine.reshape(1, rows), tokens, cotangent, w_gate, w_up, w_down_t)
 
 
 def from_partner(block, axis, distance):
@@ -133,6 +542,8 @@
         P(None, ("loop", "hid")),
     )
     out_specs = (P(("groups", "loop"), "hid"), P(("groups", "loop"), "hid"))
+    sizes = dict(mesh.shape)
+    short = sizes["groups"] == 2 and sizes["hid"] == 2 and sizes["loop"] == 8
     return jax.shard_map(
-        on_device, mesh=mesh, in_specs=in_specs, out_specs=out_specs, check_vma=False
+        on_line if short else on_device, mesh=mesh, in_specs=in_specs, out_specs=out_specs, check_vma=False
     )

time: 398 us -> 125 us (0.31)
  waiting for transfers between devices: 254 us -> 0 us
  Pallas kernels: 0 us -> 115 us
  other arithmetic: 62.3 us -> 0 us
  local copies, waits for them, and re-layouts: 36 us -> 8.48 us
  between operations: 14.7 us -> 0.65 us
  matrix products: 13 us -> 0 us
  starting transfers between devices: 12.5 us -> 0 us
  loops' own time: 5.47 us -> 0 us
    ppermute x5 -> x0, waiting for transfers between devices: 246 us -> none  [the longest x4 133 us: from_partner(): return lax.ppermute(block, axis, route)]
    pallas_call x0 -> x1, Pallas kernels: none -> 115 us  [on_line(): pl.pallas_call(functools.partial(line_kernel, line), out_shape=(out, out)...]
    dynamic_update_slice x6 -> x0, other arithmetic: 24.5 us -> none  [compute(): lax.dynamic_update_slice_in_dim(current, previous + jnp.stack([output_par...]
    slice x6 -> x0, local copies, waits for them, and re-layouts: 20.1 us -> none  [compute(): scaled = lax.dynamic_slice_in_dim(group_rows[1], start, BLOCK, 0)]
    select_n x3 -> x0, other arithmetic: 17.1 us -> none  [the longest x2 13.7 us: on_device(): jnp.where(upper_bit == 0, jnp.concatenate([group_rows, partner], 1), jnp....]
    dot_general x36 -> x0, matrix products: 13 us -> none  [the longest x6 2.21 us: compute(): lax.dot_general(grad_gate, weight_gate, contract, preferred_element_type=...]
    ppermute x5 -> x0, starting transfers between devices: 12.5 us -> none  [the longest x4 9.91 us: from_partner(): return lax.ppermute(block, axis, route)]
    convert_element_type x5 -> x0, other arithmetic: 12.2 us -> none  [the longest x1 8.14 us: on_device(): rounded = totals.astype(jnp.bfloat16)]
  transfers between devices with their start and end apart: 6 -> 0, of which waited for: 5 -> 0; matrix products, arithmetic and copies ran while one was open for 1% -> 0% of each run, Pallas kernels for 0% -> 0%
where the time goes in v1:
time: 125 us; the launch traced here: 124 us
  Pallas kernels  115 us (92%)
  local copies, waits for them, and re-layouts  8.48 us (7%)
    pallas_call x1, Pallas kernels, on_line(): pl.pallas_call(functools.partial(line_kernel, line), out_shape=(out, out)...  115 us
    unnamed x17, local copies, waits for them, and re-layouts  8.48 us

profile of v1, /device:TPU:0, one launch (start us, length us, event | category | flops | bytes accessed | tf_op | source)
XLA Modules:
  0.0 124.2 jit_solution(18177392937769445151)
XLA Ops:
  0.6 0.0 copy-start.6
  0.6 0.7 copy-done.6
  1.3 0.0 copy-start.5
  1.3 0.1 copy.9.route_ref
  1.4 0.6 copy-done.5
  2.0 0.0 copy-start
  2.0 1.1 copy-done
  3.1 0.0 copy-start.1
  3.1 1.1 copy-done.1
  4.2 0.0 copy-start.2
  4.2 1.1 copy-done.2
  5.4 0.0 copy-start.3
  5.4 1.1 copy-done.3
  6.5 0.0 copy-start.4
  6.5 1.1 copy-done.4
  7.6 115.1 %shard_map.86 = (bf16[128,1536]{1,0:T(8,128)(2,1)S(1)}, bf16[128,1536]{1,0:T(8,128)(2,1)S(1)}) custom-call(s32[8,2]{1,0:T(8,128)S(1)} %copy.9.route_ref, f32[1,128]{1,0:T(1,128)S(1)} %bitcast.1, bf16[128,3072]{1,0:T(8,128)(2,1)S(1)} %copy-done, bf16[128,3072]{1,0:T(8,128)(2,1)S(1)} %copy-done.1, bf16[3072,128]{1,0:T(8,128)(2,1)S(1)} %copy-done.2, ...), custom_call_target="tpu_custom_call" | custom-call | flops 4831838208 | bytes 4718592 | tf_op jit(solution)/shard_map/pallas_call | solution.py:374
  122.7 0.7 copy.12
  123.5 0.7 copy.13
Async XLA Ops:
  0.6 0.7 copy-start.6
  1.3 0.7 copy-start.5
  2.0 1.1 copy-start
  3.1 1.1 copy-start.1
  4.2 1.1 copy-start.2
  5.4 1.1 copy-start.3
  6.5 1.1 copy-start.4

commit v2 on v1

--- a/solution.py
+++ b/solution.py
@@ -15,10 +15,10 @@
 def line_kernel(
     line, route_ref, combine_ref, tokens_ref, cotangent_ref, gate_ref, up_ref, down_ref,
     mixed_ref, grad_ref,
-    weights, rows_in, cotan, hidden, sums, from_left, from_right, total, swap_out, swap_in,
+    weights, rows_in, cotan, hidden, sums, arrived, total, swap_out, swap_in,
     own_sem, gather_send, gather_recv,
     sibling_send, sibling_recv, side_send, side_recv, cross_send, cross_recv,
-    relay_send, relay_recv, left_send, left_recv, right_recv, swap_send, swap_recv,
+    relay_send, relay_recv, sums_send, sums_recv, swap_send, swap_recv,
 ):
     group = lax.axis_index("groups")
     loop = lax.axis_index("loop")
@@ -176,7 +176,7 @@
 
     contract = (((1,), (1,)), ((), ()))
 
-    def terms(block):
+    def terms(block, ready):
         def first(t, _):
             cols = pl.ds(pl.multiple_of(t * 256, 256), 256)
             gate = jnp.dot(rows_in[block, 0], weights[0, :, cols], preferred_element_type=jnp.float32)
@@ -195,12 +195,19 @@
 
         lax.fori_loop(0, weights.shape[2] // 256, first, 0)
 
-        def second(t, _):
+        def output_tile(t, _):
             cols = pl.ds(pl.multiple_of(t * 512, 512), 512)
             output_part = lax.dot_general(
                 hidden[0], weights[2, cols, :], contract, preferred_element_type=jnp.float32
             )
             sums[block, 0, :, cols] = output_part.astype(jnp.bfloat16)
+            return 0
+
+        lax.fori_loop(0, width // 512, output_tile, 0)
+        ready(0)
+
+        def input_tile(t, _):
+            cols = pl.ds(pl.multiple_of(t * 512, 512), 512)
             input_part = lax.dot_general(
                 hidden[1], weights[0, cols, :], contract, preferred_element_type=jnp.float32
             ) + lax.dot_general(
@@ -209,86 +216,71 @@
             sums[block, 1, :, cols] = input_part.astype(jnp.bfloat16)
             return 0
 
-        lax.fori_loop(0, width // 512, second, 0)
+        lax.fori_loop(0, width // 512, input_tile, 0)
+        ready(1)
 
     def sum_copy(block, kind, part, way):
         cols = pl.ds(part * chunk, chunk)
-        target = from_right if way == 0 else from_left
-        recv = right_recv if way == 0 else left_recv
         return remote(
-            sums.at[block, kind, :, cols], target.at[block, kind, :, cols],
-            left_send.at[block, kind, part], recv.at[block, kind, part],
-            left if way == 0 else right,
+            sums.at[block, kind, :, cols], arrived.at[way, block, kind, :, cols],
+            sums_send.at[block, kind, part], sums_recv.at[way, block, kind, part],
+            {"loop": loop + 4 * way - 2},
         )
 
     quarters = [(kind, part) for kind in range(2) for part in range(2)]
+    low = place < line // 2
+    at_end = jnp.logical_not(has_left & has_right)
+    depth = jnp.where(low, place, line - 1 - place)
+    onward_way = jnp.where(low, 1, 0)
+
+    def mirrored(block):
+        return jnp.where(low, block, line - 1 - block)
 
     def one_block(index, _):
-        distance = (index + 2) // 2
-        way = lax.rem(index, 2)
-        apart = jnp.where(index == 2 * (line - 1), 0, distance * (2 * way - 1))
-        block = place + apart
-
-        @pl.when((block >= 0) & (block < line))
-        def _():
-            @pl.when(jnp.logical_not(has_left) & (apart > 0))
+        later = jnp.where(index == 2, 3 - 3 * depth, depth)
+        block = mirrored(jnp.where(index == 0, 2, jnp.where(index == 1, 1 + 2 * depth, later)))
+
+        @pl.when(at_end & (index < line - 1))
+        def _():
+            for kind in range(2):
+                gather_copy(block, kind, 0).wait_recv()
+
+        def ready(kind):
+            @pl.when(at_end & ((index == 0) | (index == 2)))
             def _():
-                for kind in range(2):
-                    gather_copy(block, kind, 0).wait_recv()
-
-            @pl.when(jnp.logical_not(has_right) & (apart < 0))
-            def _():
-                for kind in range(2):
-                    gather_copy(block, kind, 1).wait_recv()
-
-            terms(block)
-
-            @pl.when(jnp.logical_not(has_left) & (apart > 0))
-            def _():
-                for kind, part in quarters:
-                    sum_copy(block, kind, part, 1).start()
-
-            @pl.when(jnp.logical_not(has_right) & (apart < 0))
-            def _():
-                for kind, part in quarters:
-                    sum_copy(block, kind, part, 0).start()
+                for part in range(2):
+                    sum_copy(block, kind, part, onward_way).start()
+
+        terms(block, ready)
+
+        @pl.when(at_end & (index == 2))
+        def _():
+            for kind, part in quarters:
+                sum_copy(mirrored(1), kind, part, onward_way).start()
 
         return 0
 
-    lax.fori_loop(0, 2 * (line - 1) + 1, one_block, 0)
-
-    def merge(block, kind, part, arrived):
+    lax.fori_loop(0, line, one_block, 0)
+
+    def forward(block, kind, part, way):
         cols = pl.ds(part * chunk, chunk)
+        sum_copy(block, kind, part, way).wait_recv()
         sums[block, kind, :, cols] = (
             sums[block, kind, :, cols].astype(jnp.float32)
-            + arrived[block, kind, :, cols].astype(jnp.float32)
+            + arrived[way, block, kind, :, cols].astype(jnp.float32)
         ).astype(jnp.bfloat16)
-
-    def forward(block, kind, part, way):
-        sum_copy(block, kind, part, way).wait_recv()
-        merge(block, kind, part, from_left if way == 1 else from_right)
         sum_copy(block, kind, part, way).start()
 
-    low = place < line // 2
-
-    def onward(turn, _):
-        to_right = has_left & (turn > place)
-        to_left = has_right & (line - 1 - turn < place)
-        for kind, part in quarters:
-            @pl.when(to_right & low)
-            def _():
-                forward(turn, kind, part, 1)
-
-            @pl.when(to_left)
-            def _():
-                forward(line - 1 - turn, kind, part, 0)
-
-            @pl.when(to_right & jnp.logical_not(low))
-            def _():
-                forward(turn, kind, part, 1)
-        return 0
-
-    lax.fori_loop(1, line, onward, 0)
+    @pl.when(has_left & has_right)
+    def _():
+        def onward(turn, _):
+            block = mirrored(jnp.where(turn == 0, 2, jnp.where(turn == 1, 3, 0)))
+            way = jnp.where(turn == 2, 1 - onward_way, onward_way)
+            for kind, part in quarters:
+                forward(block, kind, part, way)
+            return 0
+
+        lax.fori_loop(0, 3, onward, 0)
 
     outputs = (mixed_ref, grad_ref)
 
@@ -305,12 +297,12 @@
             @pl.when(has_left)
             def _():
                 sum_copy(place, kind, part, 1).wait_recv()
-                total[...] += from_left[place, kind, :, cols].astype(jnp.float32)
+                total[...] += arrived[1, place, kind, :, cols].astype(jnp.float32)
 
             @pl.when(has_right)
             def _():
                 sum_copy(place, kind, part, 0).wait_recv()
-                total[...] += from_right[place, kind, :, cols].astype(jnp.float32)
+                total[...] += arrived[0, place, kind, :, cols].astype(jnp.float32)
 
             value = total[...]
             if kind == 0:
@@ -365,7 +357,7 @@
     units = w_gate.shape[1]
     half = rows // 2
     line = lax.axis_size("loop") // 2
-    any_space = pl.BlockSpec(memory_space=pl.ANY)
+    any_space = pl.BlockSpec(memory_space=pltpu.HBM)
     vmem = pl.BlockSpec(memory_space=pltpu.VMEM)
     bf16 = jnp.bfloat16
     dma = pltpu.SemaphoreType.DMA
@@ -382,8 +374,7 @@
             pltpu.VMEM((half, width), bf16),
             pltpu.VMEM((3, half, 4 * units), bf16),
             pltpu.VMEM((line, 2, half, width), bf16),
-            pltpu.VMEM((line, 2, half, width), bf16),
-            pltpu.VMEM((line, 2, half, width), bf16),
+            pltpu.VMEM((2, line, 2, half, width), bf16),
             pltpu.VMEM((half, width // 2), jnp.float32),
             pltpu.VMEM((2, half, width // 2), bf16),
             pltpu.VMEM((2, half, width // 2), bf16),
@@ -399,13 +390,12 @@
             dma((2, 3, pieces)),
             dma((2, 3, pieces)),
             dma((line, 2, 2)),
-            dma((line, 2, 2)),
-            dma((line, 2, 2)),
+            dma((2, line, 2, 2)),
             dma((2,)),
             dma((2,)),
         ],
         compiler_params=pltpu.CompilerParams(
-            collective_id=0, has_side_effects=True, vmem_limit_bytes=48 * 1024 * 1024
+            collective_id=0, has_side_effects=True, vmem_limit_bytes=62 * 1024 * 1024
         ),
         cost_estimate=pl.CostEstimate(
             flops=12 * line * half * width * 4 * units,

time: 125 us -> 115 us (0.920)
  Pallas kernels: 115 us -> 110 us
  local copies, waits for them, and re-layouts: 8.48 us -> 3.91 us
    pallas_call x1, Pallas kernels: 115 us -> 110 us  [on_line(): pl.pallas_call(functools.partial(line_kernel, line), out_shape=(out, out)...]
    unnamed x17 -> x7, local copies, waits for them, and re-layouts: 8.48 us -> 3.91 us
where the time goes in v2:
time: 115 us
  Pallas kernels  110 us (96%)
  local copies, waits for them, and re-layouts  3.91 us (3%)
    pallas_call x1, Pallas kernels, on_line(): pl.pallas_call(functools.partial(line_kernel, line), out_shape=(out, out)...  110 us
    unnamed x7, local copies, waits for them, and re-layouts  3.91 us

profile of v2, /device:TPU:0, one launch (start us, length us, event | category | flops | bytes accessed | tf_op | source)
XLA Modules:
  0.0 114.9 jit_solution(14613225873231085782)
XLA Ops:
  0.6 0.0 copy-start.1
  0.6 0.7 copy-done.1
  1.3 0.7 copy.9.route_ref
  2.0 110.3 %shard_map.86 = (bf16[128,1536]{1,0:T(8,128)(2,1)}, bf16[128,1536]{1,0:T(8,128)(2,1)}) custom-call(s32[8,2]{1,0:T(8,128)} %copy.9.route_ref, f32[1,128]{1,0:T(1,128)} %bitcast.1, bf16[128,3072]{1,0:T(8,128)(2,1)} %tokens_ref.1, bf16[128,3072]{1,0:T(8,128)(2,1)} %cotangent_ref.1, bf16[3072,128]{1,0:T(8,128)(2,1)} %gate_ref.1, bf16[3072,128]{1,0:T(8,128)(2,1)} %up_ref.1, ...), custom_call_target="tpu_custom_call" | custom-call | flops 4831838208 | bytes 4718592 | tf_op jit(solution)/shard_map/pallas_call | solution.py:366
  112.3 0.0 copy-start
  112.3 1.8 %copy.12 = bf16[128,1536]{1,0:T(8,128)(2,1)} copy(bf16[128,1536]{1,0:T(8,128)(2,1)} %get-tuple-element.4) | data formatting | bytes 786432
  114.1 0.0 copy-done
  114.1 0.7 copy.13
Async XLA Ops:
  0.6 0.7 copy-start.1
  112.3 1.8 %copy-start = (bf16[128,1536]{1,0:T(8,128)(2,1)S(1)}, bf16[128,1536]{1,0:T(8,128)(2,1)}, u32[]{:S(2)}) copy-start(bf16[128,1536]{1,0:T(8,128)(2,1)} %get-tuple-element.5) | copy-start | bytes 1179652

commit v3 on v2

--- a/solution.py
+++ b/solution.py
@@ -176,14 +176,14 @@
 
     contract = (((1,), (1,)), ((), ()))
 
-    def terms(block, ready):
+    def terms(blocks, ready):
         def first(t, _):
             cols = pl.ds(pl.multiple_of(t * 256, 256), 256)
-            gate = jnp.dot(rows_in[block, 0], weights[0, :, cols], preferred_element_type=jnp.float32)
-            upward = jnp.dot(rows_in[block, 0], weights[1, :, cols], preferred_element_type=jnp.float32)
-            grad_hidden = jnp.dot(
-                rows_in[block, 1], weights[2, :, cols], preferred_element_type=jnp.float32
-            )
+            inputs = jnp.concatenate([rows_in[b, 0] for b in blocks], axis=0)
+            scaled = jnp.concatenate([rows_in[b, 1] for b in blocks], axis=0)
+            gate = jnp.dot(inputs, weights[0, :, cols], preferred_element_type=jnp.float32)
+            upward = jnp.dot(inputs, weights[1, :, cols], preferred_element_type=jnp.float32)
+            grad_hidden = jnp.dot(scaled, weights[2, :, cols], preferred_element_type=jnp.float32)
             sigma = jax.nn.sigmoid(gate)
             active = gate * sigma
             hidden[0, :, cols] = (active * upward).astype(jnp.bfloat16)
@@ -195,12 +195,15 @@
 
         lax.fori_loop(0, weights.shape[2] // 256, first, 0)
 
+        def keep(kind, cols, value):
+            for i, b in enumerate(blocks):
+                sums[b, kind, :, cols] = value[i * half:(i + 1) * half].astype(jnp.bfloat16)
+
         def output_tile(t, _):
             cols = pl.ds(pl.multiple_of(t * 512, 512), 512)
-            output_part = lax.dot_general(
+            keep(0, cols, lax.dot_general(
                 hidden[0], weights[2, cols, :], contract, preferred_element_type=jnp.float32
-            )
-            sums[block, 0, :, cols] = output_part.astype(jnp.bfloat16)
+            ))
             return 0
 
         lax.fori_loop(0, width // 512, output_tile, 0)
@@ -208,12 +211,11 @@
 
         def input_tile(t, _):
             cols = pl.ds(pl.multiple_of(t * 512, 512), 512)
-            input_part = lax.dot_general(
+            keep(1, cols, lax.dot_general(
                 hidden[1], weights[0, cols, :], contract, preferred_element_type=jnp.float32
             ) + lax.dot_general(
                 hidden[2], weights[1, cols, :], contract, preferred_element_type=jnp.float32
-            )
-            sums[block, 1, :, cols] = input_part.astype(jnp.bfloat16)
+            ))
             return 0
 
         lax.fori_loop(0, width // 512, input_tile, 0)
@@ -235,32 +237,6 @@
 
     def mirrored(block):
         return jnp.where(low, block, line - 1 - block)
-
-    def one_block(index, _):
-        later = jnp.where(index == 2, 3 - 3 * depth, depth)
-        block = mirrored(jnp.where(index == 0, 2, jnp.where(index == 1, 1 + 2 * depth, later)))
-
-        @pl.when(at_end & (index < line - 1))
-        def _():
-            for kind in range(2):
-                gather_copy(block, kind, 0).wait_recv()
-
-        def ready(kind):
-            @pl.when(at_end & ((index == 0) | (index == 2)))
-            def _():
-                for part in range(2):
-                    sum_copy(block, kind, part, onward_way).start()
-
-        terms(block, ready)
-
-        @pl.when(at_end & (index == 2))
-        def _():
-            for kind, part in quarters:
-                sum_copy(mirrored(1), kind, part, onward_way).start()
-
-        return 0
-
-    lax.fori_loop(0, line, one_block, 0)
 
     def forward(block, kind, part, way):
         cols = pl.ds(part * chunk, chunk)
@@ -271,16 +247,52 @@
         ).astype(jnp.bfloat16)
         sum_copy(block, kind, part, way).start()
 
-    @pl.when(has_left & has_right)
+    def two_blocks(index, _):
+        ahead = mirrored(jnp.where(index == 0, 2, 3 - 3 * depth))
+        behind = mirrored(jnp.where(index == 0, 1 + 2 * depth, depth))
+
+        @pl.when(at_end)
+        def _():
+            for kind in range(2):
+                gather_copy(ahead, kind, 0).wait_recv()
+
+        @pl.when(at_end & (index == 0))
+        def _():
+            for kind in range(2):
+                gather_copy(behind, kind, 0).wait_recv()
+
+        def ready(kind):
+            @pl.when(at_end)
+            def _():
+                for part in range(2):
+                    sum_copy(ahead, kind, part, onward_way).start()
+
+        terms((ahead, behind), ready)
+
+        @pl.when(at_end & (index == 1))
+        def _():
+            for kind, part in quarters:
+                sum_copy(mirrored(1), kind, part, onward_way).start()
+
+        @pl.when(jnp.logical_not(at_end))
+        def _():
+            for part in range(2):
+                forward(mirrored(2), index, part, onward_way)
+
+        return 0
+
+    lax.fori_loop(0, 2, two_blocks, 0)
+
+    @pl.when(jnp.logical_not(at_end))
     def _():
         def onward(turn, _):
-            block = mirrored(jnp.where(turn == 0, 2, jnp.where(turn == 1, 3, 0)))
-            way = jnp.where(turn == 2, 1 - onward_way, onward_way)
+            block = mirrored(3 - 3 * turn)
+            way = jnp.where(turn == 1, 1 - onward_way, onward_way)
             for kind, part in quarters:
                 forward(block, kind, part, way)
             return 0
 
-        lax.fori_loop(0, 3, onward, 0)
+        lax.fori_loop(0, 2, onward, 0)
 
     outputs = (mixed_ref, grad_ref)
 
@@ -372,7 +384,7 @@
             pltpu.VMEM((3, width, 4 * units), bf16),
             pltpu.VMEM((line, 2, half, width), bf16),
             pltpu.VMEM((half, width), bf16),
-            pltpu.VMEM((3, half, 4 * units), bf16),
+            pltpu.VMEM((3, 2 * half, 4 * units), bf16),
             pltpu.VMEM((line, 2, half, width), bf16),
             pltpu.VMEM((2, line, 2, half, width), bf16),
             pltpu.VMEM((half, width // 2), jnp.float32),

time: 115 us -> 104 us (0.904)
  Pallas kernels: 110 us -> 99 us
    pallas_call x1, Pallas kernels: 110 us -> 99 us  [on_line(): pl.pallas_call(functools.partial(line_kernel, line), out_shape=(out, out)...]
where the time goes in v3:
time: 104 us
  Pallas kernels  99 us (95%)
  local copies, waits for them, and re-layouts  3.91 us (4%)
    pallas_call x1, Pallas kernels, on_line(): pl.pallas_call(functools.partial(line_kernel, line), out_shape=(out, out)...  99 us
    unnamed x7, local copies, waits for them, and re-layouts  3.91 us

profile of v3, /device:TPU:0, one launch (start us, length us, event | category | flops | bytes accessed | tf_op | source)
XLA Modules:
  0.0 103.5 jit_solution(9004000605697353436)
XLA Ops:
  0.6 0.0 copy-start.1
  0.6 0.7 copy-done.1
  1.3 0.7 copy.9.route_ref
  2.0 99.0 %shard_map.86 = (bf16[128,1536]{1,0:T(8,128)(2,1)}, bf16[128,1536]{1,0:T(8,128)(2,1)}) custom-call(s32[8,2]{1,0:T(8,128)} %copy.9.route_ref, f32[1,128]{1,0:T(1,128)} %bitcast.1, bf16[128,3072]{1,0:T(8,128)(2,1)} %tokens_ref.1, bf16[128,3072]{1,0:T(8,128)(2,1)} %cotangent_ref.1, bf16[3072,128]{1,0:T(8,128)(2,1)} %gate_ref.1, bf16[3072,128]{1,0:T(8,128)(2,1)} %up_ref.1, ...), custom_call_target="tpu_custom_call" | custom-call | flops 4831838208 | bytes 4718592 | tf_op jit(solution)/shard_map/pallas_call | solution.py:378
  101.0 0.0 copy-start
  101.0 1.8 %copy.12 = bf16[128,1536]{1,0:T(8,128)(2,1)} copy(bf16[128,1536]{1,0:T(8,128)(2,1)} %get-tuple-element.4) | data formatting | bytes 786432
  102.8 0.0 copy-done
  102.8 0.7 copy.13
Async XLA Ops:
  0.6 0.7 copy-start.1
  101.0 1.8 %copy-start = (bf16[128,1536]{1,0:T(8,128)(2,1)S(1)}, bf16[128,1536]{1,0:T(8,128)(2,1)}, u32[]{:S(2)}) copy-start(bf16[128,1536]{1,0:T(8,128)(2,1)} %get-tuple-element.5) | copy-start | bytes 1179652

commit v4 on v3

--- a/solution.py
+++ b/solution.py
@@ -285,14 +285,11 @@
 
     @pl.when(jnp.logical_not(at_end))
     def _():
-        def onward(turn, _):
-            block = mirrored(3 - 3 * turn)
-            way = jnp.where(turn == 1, 1 - onward_way, onward_way)
-            for kind, part in quarters:
-                forward(block, kind, part, way)
-            return 0
-
-        lax.fori_loop(0, 2, onward, 0)
+        for step in range(len(quarters) + 1):
+            if step < len(quarters):
+                forward(mirrored(3), *quarters[step], onward_way)
+            if step >= 1:
+                forward(mirrored(0), *quarters[step - 1], 1 - onward_way)
 
     outputs = (mixed_ref, grad_ref)
 

time: 104 us -> 102 us (0.981); the launches traced: 104 us -> 100 us
  Pallas kernels: 99 us -> 95.6 us
    pallas_call x1, Pallas kernels: 99 us -> 95.6 us  [on_line(): pl.pallas_call(functools.partial(line_kernel, line), out_shape=(out, out)...]
where the time goes in v4:
time: 102 us; the launch traced here: 100 us
  Pallas kernels  95.6 us (94%)
  local copies, waits for them, and re-layouts  3.91 us (4%)
    pallas_call x1, Pallas kernels, on_line(): pl.pallas_call(functools.partial(line_kernel, line), out_shape=(out, out)...  95.6 us
    unnamed x7, local copies, waits for them, and re-layouts  3.91 us

profile of v4, /device:TPU:0, one launch (start us, length us, event | category | flops | bytes accessed | tf_op | source)
XLA Modules:
  0.0 100.2 jit_solution(9558322292149777114)
XLA Ops:
  0.6 0.0 copy-start.1
  0.6 0.7 copy-done.1
  1.3 0.7 copy.9.route_ref
  2.0 95.6 %shard_map.86 = (bf16[128,1536]{1,0:T(8,128)(2,1)}, bf16[128,1536]{1,0:T(8,128)(2,1)}) custom-call(s32[8,2]{1,0:T(8,128)} %copy.9.route_ref, f32[1,128]{1,0:T(1,128)} %bitcast.1, bf16[128,3072]{1,0:T(8,128)(2,1)} %tokens_ref.1, bf16[128,3072]{1,0:T(8,128)(2,1)} %cotangent_ref.1, bf16[3072,128]{1,0:T(8,128)(2,1)} %gate_ref.1, bf16[3072,128]{1,0:T(8,128)(2,1)} %up_ref.1, ...), custom_call_target="tpu_custom_call" | custom-call | flops 4831838208 | bytes 4718592 | tf_op jit(solution)/shard_map/pallas_call | solution.py:375
  97.6 0.0 copy-start
  97.6 1.8 %copy.12 = bf16[128,1536]{1,0:T(8,128)(2,1)} copy(bf16[128,1536]{1,0:T(8,128)(2,1)} %get-tuple-element.4) | data formatting | bytes 786432
  99.4 0.0 copy-done
  99.4 0.7 copy.13
Async XLA Ops:
  0.6 0.7 copy-start.1
  97.6 1.8 %copy-start = (bf16[128,1536]{1,0:T(8,128)(2,1)S(1)}, bf16[128,1536]{1,0:T(8,128)(2,1)}, u32[]{:S(2)}) copy-start(bf16[128,1536]{1,0:T(8,128)(2,1)} %get-tuple-element.5) | copy-start | bytes 1179652
